TPU v7x, 128 devices: a whole 4x4x4 slice. The times are simulated.
128 devices in a mesh: row: 8 (over x, core), col: 16 (over y, z).
Axes of the slice: x: 4, y: 4, z: 4, core: 2. Of those that a mesh axis runs over, the one named last changes fastest.
Arguments:
- nodes: bfloat16 [8192, 512], P(('row', 'col')), may hold values from -6 to 6
- edges: bfloat16 [8, 16, 4096, 512], P('row', 'col'), may hold values from -6 to 6
- senders: int32 [8, 16, 4096], P('row', 'col'), may hold values from 0 to 511
- receivers: int32 [8, 16, 4096], P('row', 'col'), may hold values from 0 to 1023
- levels: int32 [8, 16, 4096], P('row', 'col'), may hold values from 0 to 6
- counts: int32 [8, 16], P('row', 'col'), may hold values from 1 to 4096, as said below
- edge_w1: bfloat16 [3, 512, 512], replicated, may hold values from -0.15625 to 0.15625
- level_bias: bfloat16 [7, 512], replicated, may hold values from -6 to 6
- edge_w2: bfloat16 [512, 512], replicated, may hold values from -0.25 to 0.25
- edge_gain: float32 [512], replicated, may hold values from 0.1 to 1.9
- node_w1: bfloat16 [2, 512, 512], replicated, may hold values from -0.1875 to 0.1875
- node_w2: bfloat16 [512, 512], replicated, may hold values from -0.25 to 0.25
- node_gain: float32 [512], replicated, may hold values from 0.1 to 1.9
- grid: bfloat16 [131072, 512], P(('row', 'col')), may hold values from -6 to 6
- send_rows: int32 [128, 128, 4], P(('row', 'col')), may hold values from 0 to 63, as said below
- dec_index: int32 [131072, 3], P(('row', 'col')), may hold values from 0 to 511, as said below
- dec_w1: bfloat16 [2, 512, 512], replicated, may hold values from -0.1875 to 0.1875
- dec_w2: bfloat16 [512, 512], replicated, may hold values from -0.25 to 0.25
- dec_gain: float32 [512], replicated, may hold values from 0.1 to 1.9
Outputs:
- nodes_out: bfloat16 [8192, 512], P(('row', 'col'))
- edges_out: bfloat16 [8, 16, 4096, 512], P('row', 'col')
- grid_out: bfloat16 [131072, 512], P(('row', 'col'))
Inputs may be any that keep to these rules, and one draw needn't show every extreme that they name: `senders`: at slots at or beyond the tile's count the index is arbitrary and unused. `receivers`: at slots at or beyond the tile's count the index is arbitrary and unused. `counts`: some tile is full in every draw. `send_rows`: the 4 rows that one device sends to one band device are distinct. `dec_index`: buffer rows are laid out by source device, then slot; every row of a band's buffer is named by some decoder edge of that band.
All inputs are finite; a program needn't handle non-finite values.
Results may differ from a plain program's by a relative error of at most 0.015.
Values may be sent and summed in bfloat16 or wider, within the bound.
No kernel may reach another device: no remote copies, remote signals or barrier semaphores. Data moves between devices by JAX's collectives and lax.ppermute only.
A program may use at most 128 MiB of HBM per device.

v0:
```python
import math
import jax
import jax.numpy as jnp
from jax import lax
from jax.sharding import PartitionSpec as P

EPSILON = 1e-05


def layer_norm(values, gain):
    center = values - jnp.mean(values, axis=-1, keepdims=True)
    spread = jnp.mean(center * center, axis=-1, keepdims=True)
    return center * lax.rsqrt(spread + EPSILON) * gain


def mlp_tail(pre, second_weight, gain):
    hidden = jax.nn.silu(pre).astype(jnp.bfloat16)
    output = jnp.dot(hidden, second_weight, preferred_element_type=jnp.float32)
    return layer_norm(output, gain)


def one_hot_rows(ids, count):
    return (ids[:, None] == jnp.arange(count, dtype=jnp.int32)[None, :]).astype(jnp.bfloat16)


def select_low(table_hot, table):
    return jnp.dot(table_hot, table, preferred_element_type=jnp.float32).astype(jnp.bfloat16)


def on_device(
    nodes,
    edges,
    senders,
    receivers,
    levels,
    counts,
    edge_w1,
    level_bias,
    edge_w2,
    edge_gain,
    node_w1,
    node_w2,
    node_gain,
    grid,
    send_rows,
    dec_index,
    dec_w1,
    dec_w2,
    dec_gain,
):
    node_block = nodes.shape[0]
    width = nodes.shape[1]
    capacity = edges.shape[2]
    level_count = level_bias.shape[0]
    sender_count = node_block * lax.axis_size("row")
    receiver_count = node_block * lax.axis_size("col")
    sender_block = lax.all_gather(nodes, "row", axis=0, tiled=True)
    receiver_block = lax.all_gather(nodes, "col", axis=0, tiled=True)
    joined_weight = edge_w1.reshape(3 * width, width)

    def first_layer(rows, send_hot, recv_hot):
        joined = jnp.concatenate(
            [rows, select_low(send_hot, sender_block), select_low(recv_hot, receiver_block)], axis=1
        )
        return jnp.dot(joined, joined_weight, preferred_element_type=jnp.float32)

    block_rows = math.gcd(capacity, 1024)
    block_count = capacity // block_rows
    slot_used = jnp.arange(capacity, dtype=jnp.int32) < counts[0, 0]
    items = (
        edges[0, 0].reshape(block_count, block_rows, width),
        senders[0, 0].reshape(block_count, block_rows),
        receivers[0, 0].reshape(block_count, block_rows),
        levels[0, 0].reshape(block_count, block_rows),
        slot_used.reshape(block_count, block_rows),
    )

    def edge_block(partial_value, item):
        rows, send_ids, recv_ids, level_ids, used = item
        send_hot = one_hot_rows(send_ids, sender_count)
        recv_hot = one_hot_rows(recv_ids, receiver_count)
        pre = first_layer(rows, send_hot, recv_hot)
        pre = pre + jnp.dot(
            one_hot_rows(level_ids, level_count), level_bias, preferred_element_type=jnp.float32
        )
        message = mlp_tail(pre, edge_w2, edge_gain).astype(jnp.bfloat16)
        kept = jnp.where(used[:, None], message, jnp.zeros((), jnp.bfloat16))
        updated = (rows.astype(jnp.float32) + kept.astype(jnp.float32)).astype(jnp.bfloat16)
        partial_value = partial_value + lax.dot_general(
            recv_hot, kept, (((0,), (0,)), ((), ())), preferred_element_type=jnp.float32
        )
        return (partial_value, updated)

    partial_value, edge_new = lax.scan(
        edge_block, jnp.zeros((receiver_count, width), jnp.float32), items
    )
    edges_out = edge_new.reshape(1, 1, capacity, width)
    summed = lax.psum(partial_value.astype(jnp.bfloat16), "col").astype(jnp.float32)
    aggregated = lax.dynamic_slice_in_dim(summed, lax.axis_index("col") * node_block, node_block, 0)
    node_pre = jnp.dot(nodes, node_w1[0], preferred_element_type=jnp.float32)
    node_pre = node_pre + jnp.dot(
        aggregated.astype(jnp.bfloat16), node_w1[1], preferred_element_type=jnp.float32
    )
    nodes_out = (nodes.astype(jnp.float32) + mlp_tail(node_pre, node_w2, node_gain)).astype(
        jnp.bfloat16
    )
    peers = send_rows.shape[1]
    per_peer = send_rows.shape[2]
    picked = select_low(one_hot_rows(send_rows[0].reshape(-1), node_block), nodes_out).reshape(
        peers, per_peer, width
    )
    received = lax.all_to_all(picked, ("row", "col"), split_axis=0, concat_axis=0, tiled=True)
    cells = grid.shape[0]
    fan_count = dec_index.shape[1]
    chosen = select_low(
        one_hot_rows(dec_index.reshape(-1), peers * per_peer),
        received.reshape(peers * per_peer, width),
    )
    node_dec = jnp.dot(chosen, dec_w1[1], preferred_element_type=jnp.float32).reshape(
        cells, fan_count, width
    )
    grid_part = jnp.dot(grid, dec_w1[0], preferred_element_type=jnp.float32)
    dec_pre = grid_part[:, None, :] + node_dec
    messages = mlp_tail(dec_pre.reshape(cells * fan_count, width), dec_w2, dec_gain).reshape(
        cells, fan_count, width
    )
    grid_out = (grid.astype(jnp.float32) + jnp.sum(messages, axis=1)).astype(jnp.bfloat16)
    return (nodes_out, edges_out, grid_out)


def solution(mesh):
    return jax.shard_map(
        on_device,
        mesh=mesh,
        in_specs=(
            P(("row", "col"), None),
            P("row", "col", None, None),
            P("row", "col", None),
            P("row", "col", None),
            P("row", "col", None),
            P("row", "col"),
            P(),
            P(),
            P(),
            P(),
            P(),
            P(),
            P(),
            P(("row", "col"), None),
            P(("row", "col"), None, None),
            P(("row", "col"), None),
            P(),
            P(),
            P(),
        ),
        out_specs=(P(("row", "col"), None), P("row", "col", None, None), P(("row", "col"), None)),
        check_vma=False,
    )
```

profile of v0, /device:TPU:1, one launch (start us, length us, event | category | flops | bytes accessed | tf_op | source)
XLA Modules:
  0.0 344.8 jit_solution(2025392052135723121)
XLA Ops:
  13.4 15.0 %all_gather.6 = bf16[512,512]{1,0:T(8,128)(2,1)S(1)} all-gather(bf16[64,512]{1,0:T(8,128)(2,1)} %param.21), channel_id=1, replica_groups=mesh['row'=8,'col'=16] {'row'}, dimensions={0}, use_global_device_ids=true | all-gather | bytes 589824 | tf_op jit(solution)/shard_map/all_gather | solution.py:57
  28.4 26.4 %all-gather.2.cloned.1.call-done = bf16[1024,512]{1,0:T(8,128)(2,1)} async-done(((bf16[64,512]{1,0:T(8,128)(2,1)}), bf16[1024,512]{1,0:T(8,128)(2,1)}) %all-gather.2.cloned.1.call-update) | async-done | bytes 1048592 | tf_op jit(solution)/shard_map/all_gather | solution.py:58
  54.8 99.2 %while.13 = (s32[]{:T(128)}, f32[1024,512]{1,0:T(8,128)}, bf16[4,1024,512]{2,1,0:T(8,128)(2,1)}, s32[4,1024]{1,0:T(4,128)S(1)}, pred[4,1024]{1,0:T(4,128)(4,1)S(...) while((s32[]{:T(128)}, f32[1024,512]{1,0:T(8,128)}, ...), condition=%wide.region_3.4_spmd.clone, body=%wide.region_0.3_spmd.clone.sunk | while | flops 4866973696 | bytes 48897348 | solution.py:94
  62.1 5.2 %fusion.97 = f32[1024,512]{1,0:T(8,128)} fusion(bf16[1536,512]{1,0:T(8,128)(2,1)} %get-tuple-element.307, bf16[1024,512]{0,1:T(8,128)(2,1)} %fusion.95, bf16[1024,512]{0,1:T(8,128)(2,1)} %fusion.96, bf16[1024,512]{0,1:T(8,128)(2,1)S(1)} %bitcast.64), kind=kOutput, calls=%fused_computation.3.clone.1 | convolution fusion | flops 1620049920 | bytes 6815744 | tf_op jit(solution)/shard_map/while/body/eval_jaxpr/dot_general | solution.py:65
  72.9 3.0 select_add_fusion.2
  85.7 5.2 %fusion.97 = f32[1024,512]{1,0:T(8,128)} fusion(bf16[1536,512]{1,0:T(8,128)(2,1)} %get-tuple-element.307, bf16[1024,512]{0,1:T(8,128)(2,1)} %fusion.95, bf16[1024,512]{0,1:T(8,128)(2,1)} %fusion.96, bf16[1024,512]{0,1:T(8,128)(2,1)S(1)} %bitcast.64), kind=kOutput, calls=%fused_computation.3.clone.1 | convolution fusion | flops 1620049920 | bytes 6815744 | tf_op jit(solution)/shard_map/while/body/eval_jaxpr/dot_general | solution.py:65
  90.9 2.9 fusion.98
  96.5 4.6 %select_add_fusion.2 = f32[1024,512]{1,0:T(8,128)} fusion(f32[1024,512]{1,0:T(8,128)} %get-tuple-element.283, s32[1024]{0:T(1024)S(1)} %bitcast.67, pred[]{:T(512)S(6)} %compare.3, f32[1024,512]{0,1:T(8,128)S(1)} %get-tuple-element.264, f32[512]{0:T(512)S(1)} %copy-done.6, f32[1024]{0:T(1024)S(1)} %add_rsqrt_fusion.4, ...), kind=kOutput, calls=%fused_computation.10.clone.1 | convolution fusion | flops 1079508992 | bytes 6306817 | tf_op jit(solution)/shard_map/while/body/eval_jaxpr/dot_general | solution.py:89
  110.9 5.2 %fusion.97 = f32[1024,512]{1,0:T(8,128)} fusion(bf16[1536,512]{1,0:T(8,128)(2,1)} %get-tuple-element.307, bf16[1024,512]{0,1:T(8,128)(2,1)} %fusion.95, bf16[1024,512]{0,1:T(8,128)(2,1)} %fusion.96, bf16[1024,512]{0,1:T(8,128)(2,1)S(1)} %bitcast.64), kind=kOutput, calls=%fused_computation.3.clone.1 | convolution fusion | flops 1620049920 | bytes 6815744 | tf_op jit(solution)/shard_map/while/body/eval_jaxpr/dot_general | solution.py:65
  121.7 4.5 %select_add_fusion.2 = f32[1024,512]{1,0:T(8,128)} fusion(f32[1024,512]{1,0:T(8,128)} %get-tuple-element.283, s32[1024]{0:T(1024)S(1)} %bitcast.67, pred[]{:T(512)S(6)} %compare.3, f32[1024,512]{0,1:T(8,128)S(1)} %get-tuple-element.264, f32[512]{0:T(512)S(1)} %copy-done.6, f32[1024]{0:T(1024)S(1)} %add_rsqrt_fusion.4, ...), kind=kOutput, calls=%fused_computation.10.clone.1 | convolution fusion | flops 1079508992 | bytes 6306817 | tf_op jit(solution)/shard_map/while/body/eval_jaxpr/dot_general | solution.py:89
  136.1 5.2 %fusion.97 = f32[1024,512]{1,0:T(8,128)} fusion(bf16[1536,512]{1,0:T(8,128)(2,1)} %get-tuple-element.307, bf16[1024,512]{0,1:T(8,128)(2,1)} %fusion.95, bf16[1024,512]{0,1:T(8,128)(2,1)} %fusion.96, bf16[1024,512]{0,1:T(8,128)(2,1)S(1)} %bitcast.64), kind=kOutput, calls=%fused_computation.3.clone.1 | convolution fusion | flops 1620049920 | bytes 6815744 | tf_op jit(solution)/shard_map/while/body/eval_jaxpr/dot_general | solution.py:65
  146.9 4.6 %select_add_fusion.2 = f32[1024,512]{1,0:T(8,128)} fusion(f32[1024,512]{1,0:T(8,128)} %get-tuple-element.283, s32[1024]{0:T(1024)S(1)} %bitcast.67, pred[]{:T(512)S(6)} %compare.3, f32[1024,512]{0,1:T(8,128)S(1)} %get-tuple-element.264, f32[512]{0:T(512)S(1)} %copy-done.6, f32[1024]{0:T(1024)S(1)} %add_rsqrt_fusion.4, ...), kind=kOutput, calls=%fused_computation.10.clone.1 | convolution fusion | flops 1079508992 | bytes 6306817 | tf_op jit(solution)/shard_map/while/body/eval_jaxpr/dot_general | solution.py:89
  157.4 86.1 %all-reduce.2.cloned.1.call-done = bf16[1024,512]{1,0:T(8,128)(2,1)} async-done(((bf16[1024,512]{1,0:T(8,128)(2,1)}), bf16[1024,512]{1,0:T(8,128)(2,1)}) %all-reduce.2.cloned.1.call-update) | async-done | bytes 1048592 | tf_op jit(solution)/shard_map/psum | solution.py:98
  246.4 8.8 %all-to-all-start = ((bf16[128,4,512]{2,1,0:T(4,128)(2,1)}), bf16[128,4,512]{2,1,0:T(4,128)(2,1)S(1)}, u32[]{:S(2)}, u32[]{:S(2)}) async-start(bf16[128,4,512]{2,1,0:T(4,128)(2,1)} %reshape.80), calls=%async_computation | async-start | bytes 1048576 | tf_op jit(solution)/shard_map/all_to_all | solution.py:112
  257.8 11.3 %all-to-all-done = bf16[128,4,512]{2,1,0:T(4,128)(2,1)S(1)} async-done(((bf16[128,4,512]{2,1,0:T(4,128)(2,1)}), bf16[128,4,512]{2,1,0:T(4,128)(2,1)S(1)}, u32[]{:S(2)}, u32[]{:S(2)}) %all-to-all-start) | async-done | bytes 524320 | tf_op jit(solution)/shard_map/all_to_all | solution.py:112
  270.0 4.7 %fusion.28 = bf16[3072,512]{1,0:T(8,128)(2,1)} fusion(bf16[512,512]{1,0:T(8,128)(2,1)} %reshape.81, s32[3072]{0:T(1024)S(1)} %eq.75), kind=kOutput, calls=%fused_computation.43 | convolution fusion | flops 1613758464 | bytes 3682304 | tf_op jit(solution)/shard_map/dot_general | solution.py:27
  274.7 9.1 %dot_general.50 = bf16[1024,3,512]{2,1,0:T(4,128)(2,1)} reshape(bf16[3072,512]{1,0:T(8,128)(2,1)} %fusion.28) | data formatting | bytes 6291456 | tf_op jit(solution)/shard_map/dot_general | solution.py:119
  283.8 4.4 %broadcast_add_fusion = f32[1024,3,512]{2,0,1:T(8,128)S(1)} fusion(f32[1024,512]{1,0:T(8,128)S(1)} %fusion.36, bf16[1024,3,512]{2,1,0:T(4,128)(2,1)} %dot_general.50, bf16[2,512,512]{2,1,0:T(8,128)(2,1)} %param.37), kind=kOutput, calls=%fused_computation.47 | convolution fusion | flops 1612185600 | bytes 13107200 | tf_op jit(solution)/shard_map/dot_general | solution.py:119
  288.2 7.5 %copy.29 = f32[1024,3,512]{2,1,0:T(4,128)} copy(f32[1024,3,512]{2,0,1:T(8,128)S(1)} %broadcast_add_fusion) | data formatting | bytes 12582912 | tf_op jit(solution)/shard_map/add | solution.py:123
  295.8 10.8 %reshape.82 = f32[3072,512]{1,0:T(8,128)} reshape(f32[1024,3,512]{2,1,0:T(4,128)} %copy.29) | data formatting | bytes 12582912 | tf_op jit(solution)/shard_map/reshape | solution.py:124
  306.5 4.1 %fusion.62 = (f32[3072]{0:T(1024)S(1)}, f32[3072,512]{1,0:T(8,128)S(1)}) fusion(bf16[512,512]{1,0:T(8,128)(2,1)S(1)} %copy-done, f32[3072,512]{1,0:T(8,128)} %reshape.82), kind=kOutput, calls=%fused_computation.81 | convolution fusion | flops 1620046848 | bytes 13119488 | tf_op jit(solution)/shard_map/dot_general | solution.py:18
  312.7 3.8 %multiply_multiply_fusion = f32[3072,512]{1,0:T(8,128)} fusion(f32[3072,512]{1,0:T(8,128)S(1)} %get-tuple-element.172, f32[512]{0:T(512)S(1)} %copy-done.9, f32[3072]{0:T(1024)S(1)} %add_rsqrt_fusion.1, f32[3072]{0:T(1024)S(1)} %broadcast_multiply_fusion.1), kind=kLoop, calls=%fused_computation.38 | loop fusion | flops 4718592 | bytes 12609536 | tf_op jit(solution)/shard_map/mul | solution.py:13
  316.5 10.5 %reshape.83 = f32[1024,3,512]{2,1,0:T(4,128)} reshape(f32[3072,512]{1,0:T(8,128)} %multiply_multiply_fusion) | data formatting | bytes 12582912 | tf_op jit(solution)/shard_map/reshape | solution.py:124
  327.0 8.4 %reduce_sum.67 = f32[1024,512]{1,0:T(8,128)S(1)} reduce(f32[1024,3,512]{2,1,0:T(4,128)} %reshape.83, f32[]{:T(128)} %constant.51.clone.1), dimensions={1}, to_apply=%region_9.10 | reduce | flops 1048576 | bytes 8388612 | tf_op jit(solution)/shard_map/reduce_sum | solution.py:127
  (146 shorter events, 78.4 us)
Async XLA Ops:
  7.2 299.4 %copy-start = (bf16[512,512]{1,0:T(8,128)(2,1)S(1)}, bf16[512,512]{1,0:T(8,128)(2,1)}, u32[]{:S(2)}) copy-start(bf16[512,512]{1,0:T(8,128)(2,1)} %param.38) | copy-start | bytes 1572868
  7.2 47.6 %all-gather.2.cloned.1.call-start = ((), (), s32[]{:S(2)}) async-start(), calls=%async_computation.1 | async-start | bytes 1114112 | tf_op jit(solution)/shard_map/all_gather | solution.py:58
  7.9 235.5 %all-reduce.2.cloned.1.call-start = ((), (), s32[]{:S(2)}) async-start(), calls=%async_computation.2 | async-start | bytes 2097152 | tf_op jit(solution)/shard_map/psum | solution.py:98
  54.8 2.0 copy-start.11
  62.1 5.2 %copy-start.13 = (bf16[7,512]{1,0:T(8,128)(2,1)S(1)}, bf16[7,512]{1,0:T(8,128)(2,1)}, u32[]{:S(2)}) copy-start(bf16[7,512]{1,0:T(8,128)(2,1)} %get-tuple-element.309) | copy-start | bytes 21508 | tf_op jit(solution)/shard_map/while
  70.2 1.2 copy-start.2
  78.4 2.0 copy-start.11
  85.7 5.2 %copy-start.13 = (bf16[7,512]{1,0:T(8,128)(2,1)S(1)}, bf16[7,512]{1,0:T(8,128)(2,1)}, u32[]{:S(2)}) copy-start(bf16[7,512]{1,0:T(8,128)(2,1)} %get-tuple-element.309) | copy-start | bytes 21508 | tf_op jit(solution)/shard_map/while
  93.8 1.2 copy-start.2
  103.6 2.0 copy-start.11
  110.9 5.2 %copy-start.13 = (bf16[7,512]{1,0:T(8,128)(2,1)S(1)}, bf16[7,512]{1,0:T(8,128)(2,1)}, u32[]{:S(2)}) copy-start(bf16[7,512]{1,0:T(8,128)(2,1)} %get-tuple-element.309) | copy-start | bytes 21508 | tf_op jit(solution)/shard_map/while
  119.0 1.2 copy-start.2
  128.8 2.0 copy-start.11
  136.1 5.2 %copy-start.13 = (bf16[7,512]{1,0:T(8,128)(2,1)S(1)}, bf16[7,512]{1,0:T(8,128)(2,1)}, u32[]{:S(2)}) copy-start(bf16[7,512]{1,0:T(8,128)(2,1)} %get-tuple-element.309) | copy-start | bytes 21508 | tf_op jit(solution)/shard_map/while
  144.2 1.2 copy-start.2
  154.0 2.9 copy-start.10
  154.0 3.1 copy-start.3
  154.0 3.1 copy-start.4
  154.0 89.4 %copy-start.12 = (bf16[512,512]{1,0:T(8,128)(2,1)S(1)}, bf16[512,512]{1,0:T(8,128)(2,1)}, u32[]{:S(2)}) copy-start(bf16[512,512]{1,0:T(8,128)(2,1)} %param.32) | copy-start | bytes 1572868
  156.9 88.1 %copy-start.8 = (f32[512]{0:T(512)S(1)}, f32[512]{0:T(512)}, u32[]{:S(2)}) copy-start(f32[512]{0:T(512)} %param.33) | copy-start | bytes 6148
  157.4 97.9 %copy-start.7 = (s32[1024,3]{0,1:T(4,128)S(1)}, s32[1024,3]{0,1:T(4,128)}, u32[]{:S(2)}) copy-start(s32[1024,3]{0,1:T(4,128)} %param.36) | copy-start | bytes 36868
  245.1 12.7 %copy-start.5 = (bf16[64,512]{1,0:T(8,128)(2,1)}, bf16[64,512]{1,0:T(8,128)(2,1)S(1)}, u32[]{:S(2)}) copy-start(bf16[64,512]{1,0:T(8,128)(2,1)S(1)} %add_convert_fusion.2) | copy-start | bytes 196612
  246.4 22.7 %all-to-all-start = ((bf16[128,4,512]{2,1,0:T(4,128)(2,1)}), bf16[128,4,512]{2,1,0:T(4,128)(2,1)S(1)}, u32[]{:S(2)}, u32[]{:S(2)}) async-start(bf16[128,4,512]{2,1,0:T(4,128)(2,1)} %reshape.80), calls=%async_computation | async-start | bytes 1048576 | tf_op jit(solution)/shard_map/all_to_all | solution.py:112
  310.7 2.0 copy-start.9
  (8 other events, 8.9 us)
Sparse Core Ops, SparseCore 0:
  10.2 44.6 all-gather.1
  157.0 86.3 all-reduce.1
where the time goes:
time: 347 us; the launch traced here: 345 us
  waiting for transfers between devices  124 us (36%)
  matrix products  83.5 us (24%)
  local copies, waits for them, and re-layouts  66.4 us (19%)
  other arithmetic  31.3 us (9%)
  blocking collectives  15 us (4%)
  between operations  14.9 us (4%)
  starting transfers between devices  8.92 us (3%)
    psum x1, waiting for transfers between devices, on_device(): lax.psum(partial_value.astype(jnp.bfloat16), 'col').astype(jnp.float32)  86.1 us
    all_gather x1, waiting for transfers between devices, on_device(): receiver_block = lax.all_gather(nodes, 'col', axis=0, tiled=True)  26.4 us
    dot_general x10, matrix products, select_low(): jnp.dot(table_hot, table, preferred_element_type=jnp.float32)  22.4 us
    dot_general x4, matrix products, first_layer(): return jnp.dot(joined, joined_weight, preferred_element_type=jnp.float32)  20.7 us
    dot_general x6, matrix products, mlp_tail(): output = jnp.dot(hidden, second_weight, preferred_element_type=jnp.float32)  17.1 us
    dot_general x4, matrix products, edge_block(): lax.dot_general(recv_hot, kept, (((0,), (0,)), ((), ())), preferred_eleme...  16.6 us
    all_gather x1, blocking collectives, on_device(): sender_block = lax.all_gather(nodes, 'row', axis=0, tiled=True)  15 us
    all_to_all x1, waiting for transfers between devices, on_device(): lax.all_to_all(picked, ('row', 'col'), split_axis=0, concat_axis=0, tiled...  11.3 us
  transfers between devices with their start and end apart: 3, of which 3 were waited for; matrix products, arithmetic and copies ran while one was open for 2% of the time, Pallas kernels for 0%

commit v1 on v0

--- a/solution.py
+++ b/solution.py
@@ -55,7 +55,9 @@
     sender_count = node_block * lax.axis_size("row")
     receiver_count = node_block * lax.axis_size("col")
     sender_block = lax.all_gather(nodes, "row", axis=0, tiled=True)
-    receiver_block = lax.all_gather(nodes, "col", axis=0, tiled=True)
+    receiver_block = jnp.concatenate(
+        lax.all_to_all(jnp.stack([nodes] * lax.axis_size("col")), "col", 0, 0), axis=0
+    )
     joined_weight = edge_w1.reshape(3 * width, width)
 
     def first_layer(rows, send_hot, recv_hot):

time: 347 us -> 332 us (0.957)
  waiting for transfers between devices: 124 us -> 97.1 us
  starting transfers between devices: 8.92 us -> 17.5 us
  matrix products: 83.5 us -> 88.4 us
    all_gather x1 -> x0, waiting for transfers between devices: 26.4 us -> none  [on_device(): receiver_block = lax.all_gather(nodes, 'col', axis=0, tiled=True)]
    all_to_all x0 -> x1, starting transfers between devices: none -> 8.65 us  [on_device(): lax.all_to_all(jnp.stack([nodes] * lax.axis_size('col')), 'col', 0, 0)]
    dot_general x10, matrix products: 22.4 us -> 27.3 us  [select_low(): jnp.dot(table_hot, table, preferred_element_type=jnp.float32)]
    while x40 -> x16, local copies, waits for them, and re-layouts: 7.65 us -> 7.65 us
  transfers between devices with their start and end apart: 3 -> 3, of which waited for: 3 -> 2; matrix products, arithmetic and copies ran while one was open for 2% -> 2% of each run, Pallas kernels for 0% -> 0%
where the time goes in v1:
time: 332 us; the launch traced here: 330 us
  waiting for transfers between devices  97.1 us (29%)
  matrix products  88.4 us (27%)
  local copies, waits for them, and re-layouts  68.4 us (21%)
  other arithmetic  29 us (9%)
  starting transfers between devices  17.5 us (5%)
  between operations  15 us (5%)
  blocking collectives  14.3 us (4%)
    psum x1, waiting for transfers between devices, on_device(): lax.psum(partial_value.astype(jnp.bfloat16), 'col').astype(jnp.float32)  85.8 us
    dot_general x10, matrix products, select_low(): jnp.dot(table_hot, table, preferred_element_type=jnp.float32)  27.3 us
    dot_general x4, matrix products, first_layer(): return jnp.dot(joined, joined_weight, preferred_element_type=jnp.float32)  20.7 us
    dot_general x6, matrix products, mlp_tail(): output = jnp.dot(hidden, second_weight, preferred_element_type=jnp.float32)  17.1 us
    dot_general x4, matrix products, edge_block(): lax.dot_general(recv_hot, kept, (((0,), (0,)), ((), ())), preferred_eleme...  16.6 us
    all_gather x1, blocking collectives, on_device(): sender_block = lax.all_gather(nodes, 'row', axis=0, tiled=True)  14.3 us
    all_to_all x1, waiting for transfers between devices, on_device(): lax.all_to_all(picked, ('row', 'col'), split_axis=0, concat_axis=0, tiled...  11.3 us
    reshape x1, local copies, waits for them, and re-layouts, on_device(): dec_pre.reshape(cells * fan_count, width)  10.8 us
  transfers between devices with their start and end apart: 3, of which 2 were waited for; matrix products, arithmetic and copies ran while one was open for 2% of the time, Pallas kernels for 0%

profile of v1, /device:TPU:1, one launch (start us, length us, event | category | flops | bytes accessed | tf_op | source)
XLA Modules:
  0.0 330.0 jit_solution(6802992136860983315)
XLA Ops:
  9.2 8.6 %all-to-all-start = ((bf16[16,64,512]{2,1,0:T(8,128)(2,1)}), bf16[16,64,512]{2,1,0:T(8,128)(2,1)}, u32[]{:S(2)}, u32[]{:S(2)}) async-start(bf16[16,64,512]{2,1,0:T(8,128)(2,1)} %stack.2), calls=%async_computation | async-start | bytes 2097152 | tf_op jit(solution)/shard_map/all_to_all | solution.py:59
  21.2 14.3 %all_gather.3 = bf16[512,512]{1,0:T(8,128)(2,1)S(1)} all-gather(bf16[64,512]{1,0:T(8,128)(2,1)S(1)} %copy-done.3), channel_id=1, replica_groups=mesh['row'=8,'col'=16] {'row'}, dimensions={0}, use_global_device_ids=true | all-gather | bytes 589824 | tf_op jit(solution)/shard_map/all_gather | solution.py:57
  35.5 104.0 %while.13 = (s32[]{:T(128)}, f32[1024,512]{1,0:T(8,128)}, bf16[4,1024,512]{2,1,0:T(8,128)(2,1)}, s32[4,1024]{1,0:T(4,128)S(1)}, pred[4,1024]{1,0:T(4,128)(4,1)S(...) while((s32[]{:T(128)}, f32[1024,512]{1,0:T(8,128)}, ...), condition=%wide.region_3.4_spmd.clone, body=%wide.region_0.3_spmd.clone.sunk | while | flops 4866973696 | bytes 44666096 | solution.py:96
  44.0 5.2 %fusion.97 = f32[1024,512]{1,0:T(8,128)} fusion(bf16[1536,512]{1,0:T(8,128)(2,1)} %get-tuple-element.307, bf16[1024,512]{0,1:T(8,128)(2,1)} %fusion.95, bf16[1024,512]{0,1:T(8,128)(2,1)} %fusion.96, bf16[1024,512]{0,1:T(8,128)(2,1)S(1)} %bitcast.65), kind=kOutput, calls=%fused_computation.3.clone.1 | convolution fusion | flops 1620049920 | bytes 6815744 | tf_op jit(solution)/shard_map/while/body/eval_jaxpr/dot_general | solution.py:67
  68.8 5.2 %fusion.97 = f32[1024,512]{1,0:T(8,128)} fusion(bf16[1536,512]{1,0:T(8,128)(2,1)} %get-tuple-element.307, bf16[1024,512]{0,1:T(8,128)(2,1)} %fusion.95, bf16[1024,512]{0,1:T(8,128)(2,1)} %fusion.96, bf16[1024,512]{0,1:T(8,128)(2,1)S(1)} %bitcast.65), kind=kOutput, calls=%fused_computation.3.clone.1 | convolution fusion | flops 1620049920 | bytes 6815744 | tf_op jit(solution)/shard_map/while/body/eval_jaxpr/dot_general | solution.py:67
  79.6 4.6 %select_add_fusion.2 = f32[1024,512]{1,0:T(8,128)} fusion(f32[1024,512]{1,0:T(8,128)} %get-tuple-element.283, s32[1024]{0:T(1024)S(1)} %bitcast.68, pred[]{:T(512)S(6)} %compare.3, f32[1024,512]{0,1:T(8,128)S(1)} %get-tuple-element.264, f32[512]{0:T(512)S(1)} %get-tuple-element.311, f32[1024]{0:T(1024)S(1)} %add_rsqrt_fusion.4, ...), kind=kOutput, calls=%fused_computation.10.clone.1 | convolution fusion | flops 1079508992 | bytes 6306817 | tf_op jit(solution)/shard_map/while/body/eval_jaxpr/dot_general | solution.py:91
  88.7 3.6 %fusion.95 = bf16[1024,512]{0,1:T(8,128)(2,1)} fusion(bf16[1024,512]{1,0:T(8,128)(2,1)} %get-tuple-element.306, s32[1024]{0:T(1024)S(1)} %bitcast.67), kind=kOutput, calls=%fused_computation.20.clone.1 | convolution fusion | flops 1075314688 | bytes 2101248 | tf_op jit(solution)/shard_map/while/body/eval_jaxpr/dot_general | solution.py:27
  95.2 5.2 %fusion.97 = f32[1024,512]{1,0:T(8,128)} fusion(bf16[1536,512]{1,0:T(8,128)(2,1)} %get-tuple-element.307, bf16[1024,512]{0,1:T(8,128)(2,1)} %fusion.95, bf16[1024,512]{0,1:T(8,128)(2,1)} %fusion.96, bf16[1024,512]{0,1:T(8,128)(2,1)S(1)} %bitcast.65), kind=kOutput, calls=%fused_computation.3.clone.1 | convolution fusion | flops 1620049920 | bytes 6815744 | tf_op jit(solution)/shard_map/while/body/eval_jaxpr/dot_general | solution.py:67
  106.0 4.5 %select_add_fusion.2 = f32[1024,512]{1,0:T(8,128)} fusion(f32[1024,512]{1,0:T(8,128)} %get-tuple-element.283, s32[1024]{0:T(1024)S(1)} %bitcast.68, pred[]{:T(512)S(6)} %compare.3, f32[1024,512]{0,1:T(8,128)S(1)} %get-tuple-element.264, f32[512]{0:T(512)S(1)} %get-tuple-element.311, f32[1024]{0:T(1024)S(1)} %add_rsqrt_fusion.4, ...), kind=kOutput, calls=%fused_computation.10.clone.1 | convolution fusion | flops 1079508992 | bytes 6306817 | tf_op jit(solution)/shard_map/while/body/eval_jaxpr/dot_general | solution.py:91
  115.1 3.6 %fusion.95 = bf16[1024,512]{0,1:T(8,128)(2,1)} fusion(bf16[1024,512]{1,0:T(8,128)(2,1)} %get-tuple-element.306, s32[1024]{0:T(1024)S(1)} %bitcast.67), kind=kOutput, calls=%fused_computation.20.clone.1 | convolution fusion | flops 1075314688 | bytes 2101248 | tf_op jit(solution)/shard_map/while/body/eval_jaxpr/dot_general | solution.py:27
  121.6 5.2 %fusion.97 = f32[1024,512]{1,0:T(8,128)} fusion(bf16[1536,512]{1,0:T(8,128)(2,1)} %get-tuple-element.307, bf16[1024,512]{0,1:T(8,128)(2,1)} %fusion.95, bf16[1024,512]{0,1:T(8,128)(2,1)} %fusion.96, bf16[1024,512]{0,1:T(8,128)(2,1)S(1)} %bitcast.65), kind=kOutput, calls=%fused_computation.3.clone.1 | convolution fusion | flops 1620049920 | bytes 6815744 | tf_op jit(solution)/shard_map/while/body/eval_jaxpr/dot_general | solution.py:67
  132.4 4.5 %select_add_fusion.2 = f32[1024,512]{1,0:T(8,128)} fusion(f32[1024,512]{1,0:T(8,128)} %get-tuple-element.283, s32[1024]{0:T(1024)S(1)} %bitcast.68, pred[]{:T(512)S(6)} %compare.3, f32[1024,512]{0,1:T(8,128)S(1)} %get-tuple-element.264, f32[512]{0:T(512)S(1)} %get-tuple-element.311, f32[1024]{0:T(1024)S(1)} %add_rsqrt_fusion.4, ...), kind=kOutput, calls=%fused_computation.10.clone.1 | convolution fusion | flops 1079508992 | bytes 6306817 | tf_op jit(solution)/shard_map/while/body/eval_jaxpr/dot_general | solution.py:91
  142.8 85.8 %all-reduce.2.cloned.1.call-done = bf16[1024,512]{1,0:T(8,128)(2,1)} async-done(((bf16[1024,512]{1,0:T(8,128)(2,1)}), bf16[1024,512]{1,0:T(8,128)(2,1)}) %all-reduce.2.cloned.1.call-update) | async-done | bytes 1048592 | tf_op jit(solution)/shard_map/psum | solution.py:100
  231.6 8.8 %all-to-all-start.1 = ((bf16[128,4,512]{2,1,0:T(4,128)(2,1)}), bf16[128,4,512]{2,1,0:T(4,128)(2,1)S(1)}, u32[]{:S(2)}, u32[]{:S(2)}) async-start(bf16[128,4,512]{2,1,0:T(4,128)(2,1)} %reshape.86), calls=%async_computation.1 | async-start | bytes 1048576 | tf_op jit(solution)/shard_map/all_to_all | solution.py:114
  243.0 11.3 %all-to-all-done.1 = bf16[128,4,512]{2,1,0:T(4,128)(2,1)S(1)} async-done(((bf16[128,4,512]{2,1,0:T(4,128)(2,1)}), bf16[128,4,512]{2,1,0:T(4,128)(2,1)S(1)}, u32[]{:S(2)}, u32[]{:S(2)}) %all-to-all-start.1) | async-done | bytes 524320 | tf_op jit(solution)/shard_map/all_to_all | solution.py:114
  255.2 4.7 %fusion.28 = bf16[3072,512]{1,0:T(8,128)(2,1)} fusion(bf16[512,512]{1,0:T(8,128)(2,1)} %reshape.87, s32[3072]{0:T(1024)S(1)} %eq.75), kind=kOutput, calls=%fused_computation.43 | convolution fusion | flops 1613758464 | bytes 3682304 | tf_op jit(solution)/shard_map/dot_general | solution.py:27
  259.9 9.1 %dot_general.50 = bf16[1024,3,512]{2,1,0:T(4,128)(2,1)} reshape(bf16[3072,512]{1,0:T(8,128)(2,1)} %fusion.28) | data formatting | bytes 6291456 | tf_op jit(solution)/shard_map/dot_general | solution.py:121
  269.0 4.4 %broadcast_add_fusion = f32[1024,3,512]{2,0,1:T(8,128)S(1)} fusion(f32[1024,512]{1,0:T(8,128)S(1)} %fusion.36, bf16[1024,3,512]{2,1,0:T(4,128)(2,1)} %dot_general.50, bf16[2,512,512]{2,1,0:T(8,128)(2,1)} %param.37), kind=kOutput, calls=%fused_computation.47 | convolution fusion | flops 1612185600 | bytes 13107200 | tf_op jit(solution)/shard_map/dot_general | solution.py:121
  273.4 7.5 %copy.29 = f32[1024,3,512]{2,1,0:T(4,128)} copy(f32[1024,3,512]{2,0,1:T(8,128)S(1)} %broadcast_add_fusion) | data formatting | bytes 12582912 | tf_op jit(solution)/shard_map/add | solution.py:125
  281.0 10.8 %reshape.88 = f32[3072,512]{1,0:T(8,128)} reshape(f32[1024,3,512]{2,1,0:T(4,128)} %copy.29) | data formatting | bytes 12582912 | tf_op jit(solution)/shard_map/reshape | solution.py:126
  291.7 4.2 %fusion.62 = (f32[3072]{0:T(1024)S(1)}, f32[3072,512]{1,0:T(8,128)S(1)}) fusion(bf16[512,512]{1,0:T(8,128)(2,1)S(1)} %copy-done, f32[3072,512]{1,0:T(8,128)} %reshape.88), kind=kOutput, calls=%fused_computation.81 | convolution fusion | flops 1620046848 | bytes 13119488 | tf_op jit(solution)/shard_map/dot_general | solution.py:18
  297.9 3.8 %multiply_multiply_fusion = f32[3072,512]{1,0:T(8,128)} fusion(f32[3072,512]{1,0:T(8,128)S(1)} %get-tuple-element.172, f32[512]{0:T(512)S(1)} %copy-done.12, f32[3072]{0:T(1024)S(1)} %add_rsqrt_fusion.1, f32[3072]{0:T(1024)S(1)} %broadcast_multiply_fusion.1), kind=kLoop, calls=%fused_computation.38 | loop fusion | flops 4718592 | bytes 12609536 | tf_op jit(solution)/shard_map/mul | solution.py:13
  301.7 10.5 %reshape.89 = f32[1024,3,512]{2,1,0:T(4,128)} reshape(f32[3072,512]{1,0:T(8,128)} %multiply_multiply_fusion) | data formatting | bytes 12582912 | tf_op jit(solution)/shard_map/reshape | solution.py:126
  312.2 8.4 %reduce_sum.67 = f32[1024,512]{1,0:T(8,128)S(1)} reduce(f32[1024,3,512]{2,1,0:T(4,128)} %reshape.89, f32[]{:T(128)} %constant.51.clone.1), dimensions={1}, to_apply=%region_9.10 | reduce | flops 1048576 | bytes 8388612 | tf_op jit(solution)/shard_map/reduce_sum | solution.py:129
  (132 shorter events, 80.9 us)
Async XLA Ops:
  7.2 284.6 %copy-start = (bf16[512,512]{1,0:T(8,128)(2,1)S(1)}, bf16[512,512]{1,0:T(8,128)(2,1)}, u32[]{:S(2)}) copy-start(bf16[512,512]{1,0:T(8,128)(2,1)} %param.38) | copy-start | bytes 1572868
  7.2 14.0 %copy-start.3 = (bf16[64,512]{1,0:T(8,128)(2,1)S(1)}, bf16[64,512]{1,0:T(8,128)(2,1)}, u32[]{:S(2)}) copy-start(bf16[64,512]{1,0:T(8,128)(2,1)} %param.21) | copy-start | bytes 196612
  7.2 12.0 %copy-start.8 = (s32[1,1,4096]{2,1,0:T(1,128)S(1)}, s32[1,1,4096]{2,1,0:T(1,128)}, u32[]{:S(2)}) copy-start(s32[1,1,4096]{2,1,0:T(1,128)} %param.23) | copy-start | bytes 49156
  7.2 12.6 %copy-start.9 = (s32[1,1,4096]{2,1,0:T(1,128)S(1)}, s32[1,1,4096]{2,1,0:T(1,128)}, u32[]{:S(2)}) copy-start(s32[1,1,4096]{2,1,0:T(1,128)} %param.24) | copy-start | bytes 49156
  7.2 13.3 %copy-start.10 = (s32[1,1,4096]{2,1,0:T(1,128)S(1)}, s32[1,1,4096]{2,1,0:T(1,128)}, u32[]{:S(2)}) copy-start(s32[1,1,4096]{2,1,0:T(1,128)} %param.25) | copy-start | bytes 49156
  7.2 28.2 %copy-start.6 = (f32[512]{0:T(512)S(1)}, f32[512]{0:T(512)}, u32[]{:S(2)}) copy-start(f32[512]{0:T(512)} %param.30) | copy-start | bytes 6148
  7.2 28.2 %copy-start.15 = (bf16[7,512]{1,0:T(8,128)(2,1)S(1)}, bf16[7,512]{1,0:T(8,128)(2,1)}, u32[]{:S(2)}) copy-start(bf16[7,512]{1,0:T(8,128)(2,1)} %param.28) | copy-start | bytes 21508
  9.2 26.2 %all-to-all-start = ((bf16[16,64,512]{2,1,0:T(8,128)(2,1)}), bf16[16,64,512]{2,1,0:T(8,128)(2,1)}, u32[]{:S(2)}, u32[]{:S(2)}) async-start(bf16[16,64,512]{2,1,0:T(8,128)(2,1)} %stack.2), calls=%async_computation | async-start | bytes 2097152 | tf_op jit(solution)/shard_map/all_to_all | solution.py:59
  17.9 210.7 %all-reduce.2.cloned.1.call-start = ((), (), s32[]{:S(2)}) async-start(), calls=%async_computation.2 | async-start | bytes 2097152 | tf_op jit(solution)/shard_map/psum | solution.py:100
  43.0 1.0 copy-start.1
  52.0 1.2 copy-start.2
  67.8 1.0 copy-start.1
  76.8 1.2 copy-start.2
  94.2 1.0 copy-start.1
  103.3 1.2 copy-start.2
  129.7 1.2 copy-start.2
  139.5 2.9 copy-start.13
  139.5 3.1 copy-start.4
  139.5 89.1 %copy-start.14 = (bf16[512,512]{1,0:T(8,128)(2,1)S(1)}, bf16[512,512]{1,0:T(8,128)(2,1)}, u32[]{:S(2)}) copy-start(bf16[512,512]{1,0:T(8,128)(2,1)} %param.32) | copy-start | bytes 1572868
  142.3 87.9 %copy-start.11 = (f32[512]{0:T(512)S(1)}, f32[512]{0:T(512)}, u32[]{:S(2)}) copy-start(f32[512]{0:T(512)} %param.33) | copy-start | bytes 6148
  142.8 97.6 %copy-start.7 = (s32[1024,3]{0,1:T(4,128)S(1)}, s32[1024,3]{0,1:T(4,128)}, u32[]{:S(2)}) copy-start(s32[1024,3]{0,1:T(4,128)} %param.36) | copy-start | bytes 36868
  230.3 12.7 %copy-start.5 = (bf16[64,512]{1,0:T(8,128)(2,1)}, bf16[64,512]{1,0:T(8,128)(2,1)S(1)}, u32[]{:S(2)}) copy-start(bf16[64,512]{1,0:T(8,128)(2,1)S(1)} %add_convert_fusion.2) | copy-start | bytes 196612
  231.6 22.7 %all-to-all-start.1 = ((bf16[128,4,512]{2,1,0:T(4,128)(2,1)}), bf16[128,4,512]{2,1,0:T(4,128)(2,1)S(1)}, u32[]{:S(2)}, u32[]{:S(2)}) async-start(bf16[128,4,512]{2,1,0:T(4,128)(2,1)} %reshape.86), calls=%async_computation.1 | async-start | bytes 1048576 | tf_op jit(solution)/shard_map/all_to_all | solution.py:114
  295.9 2.0 copy-start.12
  (1 other events, 1.0 us)
Sparse Core Ops, SparseCore 0:
  142.4 86.1 all-reduce.1
